TPU v7x, 32 devices: a whole 2x2x4 slice. The times are simulated.
32 devices in a mesh: grp: 4 (over x, core), dev: 8 (over z, y).
Axes of the slice: x: 2, y: 2, z: 4, core: 2. Of those that a mesh axis runs over, the one named last changes fastest.
Arguments:
- views_a: bfloat16 [8192, 256], P(('grp', 'dev')), may hold values from -6 to 6
- views_b: bfloat16 [8192, 256], P(('grp', 'dev')), may hold values from -6 to 6
- positives: int32 [8192], P(('grp', 'dev')), may hold values from 0 to 8191, as said below
- plan: int32 [2, 4], replicated, may hold values from 0 to 3, as said below
Outputs:
- grad_a: float32 [8192, 256], P(('grp', 'dev'))
- grad_b: float32 [8192, 256], P(('grp', 'dev'))
Inputs may be any that keep to these rules, and one draw needn't show every extreme that they name: Row r holds a round of one round-robin over the 4 groups: plan[r, plan[r, g]] == g and plan[r, g] != g; no two rows pair the same two groups. positives[i] is i itself or a view of a group that plan pairs with the group of view i in some row.
All inputs are finite; a program needn't handle non-finite values.
Results may differ from a plain program's by a relative error of at most 0.00057.
Values may be sent and summed in bfloat16 or wider, within the bound.
A program may use at most 128 MiB of HBM per device.

v0:
```python
import math

import jax
import jax.numpy as jnp
from jax import lax
from jax.sharding import PartitionSpec as P

logit_scale = 2.0
logit_bias = -6.0


def weights_for(queries, labels, keys, first, factor):
    logits = (
        lax.dot_general(queries, keys, (((1,), (1,)), ((), ())), preferred_element_type=jnp.float32)
        * factor
        + logit_bias
    )
    columns = first + jnp.arange(keys.shape[0], dtype=jnp.int32)
    hit = (labels[:, None] == columns[None, :]).astype(jnp.float32)
    return (jax.nn.sigmoid(logits) - hit).astype(jnp.bfloat16)


def left_product(weights, values):
    return lax.dot_general(
        weights, values, (((0,), (0,)), ((), ())), preferred_element_type=jnp.float32
    )


def shards(views_a, views_b, positives, plan):
    rows = views_a.shape[0]
    width = views_a.shape[1]
    members = lax.axis_size("dev")
    groups = lax.axis_size("grp")
    group_rows = rows * members
    group = lax.axis_index("grp")
    factor = logit_scale / math.sqrt(width)
    partners = lax.dynamic_index_in_dim(plan, group, 1, keepdims=False)
    rounds = plan.shape[0]

    def score_group(key_shard, owner):
        first = owner * group_rows
        piece = lax.all_gather(key_shard, "dev", axis=0, tiled=True)
        weights = weights_for(views_a, positives, piece, first, factor)
        grad_rows = jnp.dot(weights, piece, preferred_element_type=jnp.float32)
        grad_keys = left_product(weights, views_a)
        grad_rows, grad_keys = (grad_rows, grad_keys)
        return (grad_rows, lax.psum_scatter(grad_keys, "dev", scatter_dimension=0, tiled=True))

    grad_a, grad_b = score_group(views_b, group)
    gathered = lax.all_gather(views_b, "grp", axis=0, tiled=True)
    returned = jnp.zeros((groups, rows, width), jnp.float32)
    for slot in range(rounds):
        partner = partners[slot]
        shard = lax.dynamic_slice_in_dim(gathered, partner * rows, rows, 0)
        grad_rows, share = score_group(shard, partner)
        grad_a = grad_a + grad_rows
        returned = lax.dynamic_update_slice(returned, share[None], (partner, 0, 0))
    back = lax.psum_scatter(returned, "grp", scatter_dimension=0, tiled=True)
    grad_b = grad_b + back[0]
    return (grad_a * factor, grad_b * factor)


def solution(mesh):
    placed = (P(("grp", "dev"), None), P(("grp", "dev"), None), P(("grp", "dev")), P())
    return jax.shard_map(
        shards,
        mesh=mesh,
        in_specs=placed,
        out_specs=(P(("grp", "dev"), None), P(("grp", "dev"), None)),
        check_vma=False,
    )
```

profile of v0, /device:TPU:0, one launch (start us, length us, event | category | flops | bytes accessed | tf_op | source)
XLA Modules:
  0.0 388.5 jit_solution(11574871856970530895)
XLA Ops:
  7.2 0.0 copy-start
  7.2 0.0 all-gather.6.cloned.1.call-start
  7.2 0.8 constant_dynamic-slice_fusion.2
  8.0 0.6 fusion.25
  9.8 8.8 %all_gather.13 = bf16[1024,256]{1,0:T(8,128)(2,1)S(1)} all-gather(bf16[256,256]{1,0:T(8,128)(2,1)} %param.5), channel_id=1, replica_groups=mesh['grp'=4,'dev'=8] {'grp'}, dimensions={0}, use_global_device_ids=true | all-gather | bytes 655360 | tf_op jit(solution)/shard_map/all_gather | solution.py:50
  18.6 0.7 constant_dynamic-slice_fusion
  19.3 0.0 all-gather.6.cloned.1.call-update
  19.4 0.0 all-gather.8.cloned.1.call-start
  19.4 0.7 all-gather.8.cloned.1.call-update
  20.1 0.0 all-gather.4.cloned.1.call-start
  20.2 0.7 all-gather.4.cloned.1.call-update
  20.9 0.0 reduce-scatter.7.cloned.1.call-start
  21.5 39.1 %all-gather.6.cloned.1.call-done = bf16[2048,256]{1,0:T(8,128)(2,1)} async-done(((bf16[256,256]{1,0:T(8,128)(2,1)}), bf16[2048,256]{1,0:T(8,128)(2,1)}) %all-gather.6.cloned.1.call-update) | async-done | bytes 1048592 | tf_op jit(solution)/shard_map/all_gather | solution.py:42
  60.6 0.0 copy-done
  60.6 2.1 fusion.18
  62.7 0.0 copy-start.3
  62.7 1.8 fusion.28
  64.5 0.0 reduce-scatter.7.cloned.1.call-update
  64.5 0.0 reduce-scatter.9.cloned.1.call-start
  65.3 36.9 %all-gather.8.cloned.1.call-done = bf16[2048,256]{1,0:T(8,128)(2,1)} async-done(((bf16[256,256]{1,0:T(8,128)(2,1)}), bf16[2048,256]{1,0:T(8,128)(2,1)}) %all-gather.8.cloned.1.call-update) | async-done | bytes 1048592 | tf_op jit(solution)/shard_map/all_gather | solution.py:42
  102.2 0.0 copy-done.3
  102.2 2.1 fusion.22
  104.3 1.8 fusion.29
  106.1 0.0 reduce-scatter.9.cloned.1.call-update
  106.1 0.0 reduce-scatter.5.cloned.1.call-start
  106.2 37.1 %all-gather.4.cloned.1.call-done = bf16[2048,256]{1,0:T(8,128)(2,1)} async-done(((bf16[256,256]{1,0:T(8,128)(2,1)}), bf16[2048,256]{1,0:T(8,128)(2,1)}) %all-gather.4.cloned.1.call-update) | async-done | bytes 1048592 | tf_op jit(solution)/shard_map/all_gather | solution.py:42
  143.3 2.1 fusion.14
  145.4 1.8 fusion.27
  147.2 0.0 reduce-scatter.5.cloned.1.call-update
  147.2 0.0 reduce-scatter.11.cloned.1.call-start
  150.9 62.1 %reduce-scatter.7.cloned.1.call-done = f32[256,256]{1,0:T(8,128)} async-done(((f32[2048,256]{1,0:T(8,128)}), f32[256,256]{1,0:T(8,128)}) %reduce-scatter.7.cloned.1.call-update) | async-done | bytes 262160 | tf_op jit(solution)/shard_map/reduce_scatter | solution.py:47
  213.0 1.1 broadcast_in_dim.6
  214.1 1.7 bitcast_dynamic-update-slice_fusion.1
  215.7 67.4 %reduce-scatter.9.cloned.1.call-done = f32[256,256]{1,0:T(8,128)} async-done(((f32[2048,256]{1,0:T(8,128)}), f32[256,256]{1,0:T(8,128)}) %reduce-scatter.9.cloned.1.call-update) | async-done | bytes 262160 | tf_op jit(solution)/shard_map/reduce_scatter | solution.py:47
  283.1 1.7 bitcast_dynamic-update-slice_fusion
  284.8 0.0 reduce-scatter.11.cloned.1.call-update
  284.8 0.0 copy-start.1
  284.8 0.0 copy-start.2
  284.8 1.8 fusion.26
  286.7 0.0 copy-done.1
  286.7 0.4 convolution_add_fusion.1
  287.1 0.0 copy-done.2
  287.1 1.2 fusion.23
  288.3 65.1 %reduce-scatter.5.cloned.1.call-done = f32[256,256]{1,0:T(8,128)} async-done(((f32[2048,256]{1,0:T(8,128)}), f32[256,256]{1,0:T(8,128)}) %reduce-scatter.5.cloned.1.call-update) | async-done | bytes 262160 | tf_op jit(solution)/shard_map/reduce_scatter | solution.py:47
  353.4 26.6 %reduce-scatter.11.cloned.1.call-done = f32[1,256,256]{2,1,0:T(8,128)} async-done(((f32[4,256,256]{2,1,0:T(8,128)}), f32[1,256,256]{2,1,0:T(8,128)}) %reduce-scatter.11.cloned.1.call-update) | async-done | bytes 262160 | tf_op jit(solution)/shard_map/reduce_scatter | solution.py:58
  379.9 1.8 fusion.24
  (3 shorter events, 0.0 us)
Async XLA Ops:
  7.2 53.4 %copy-start = (bf16[256,256]{1,0:T(8,128)(2,1)S(1)}, bf16[256,256]{1,0:T(8,128)(2,1)}, u32[]{:S(2)}) copy-start(bf16[256,256]{1,0:T(8,128)(2,1)} %param.4) | copy-start | bytes 393220
  7.2 53.4 %all-gather.6.cloned.1.call-start = ((), (), s32[]{:S(2)}) async-start(), calls=%async_computation.5 | async-start | bytes 1179648 | tf_op jit(solution)/shard_map/all_gather | solution.py:42
  19.4 82.8 %all-gather.8.cloned.1.call-start = ((), (), s32[]{:S(2)}) async-start(), calls=%async_computation.6 | async-start | bytes 1179648 | tf_op jit(solution)/shard_map/all_gather | solution.py:42
  20.1 123.1 %all-gather.4.cloned.1.call-start = ((), (), s32[]{:S(2)}) async-start(), calls=%async_computation.4 | async-start | bytes 1179648 | tf_op jit(solution)/shard_map/all_gather | solution.py:42
  20.9 192.1 %reduce-scatter.7.cloned.1.call-start = ((), (), s32[]{:S(2)}) async-start(), calls=%async_computation.8 | async-start | bytes 2359296 | tf_op jit(solution)/shard_map/reduce_scatter | solution.py:47
  62.7 39.5 %copy-start.3 = (s32[256]{0:T(256)S(1)}, s32[256]{0:T(256)}, u32[]{:S(2)}) copy-start(s32[256]{0:T(256)} %param.6) | copy-start | bytes 3076
  64.5 218.6 %reduce-scatter.9.cloned.1.call-start = ((), (), s32[]{:S(2)}) async-start(), calls=%async_computation.9 | async-start | bytes 2359296 | tf_op jit(solution)/shard_map/reduce_scatter | solution.py:47
  106.1 247.2 %reduce-scatter.5.cloned.1.call-start = ((), (), s32[]{:S(2)}) async-start(), calls=%async_computation.7 | async-start | bytes 2359296 | tf_op jit(solution)/shard_map/reduce_scatter | solution.py:47
  147.2 232.7 %reduce-scatter.11.cloned.1.call-start = ((), (), s32[]{:S(2)}) async-start(), calls=%async_computation.10 | async-start | bytes 1310720 | tf_op jit(solution)/shard_map/reduce_scatter | solution.py:58
  284.8 1.8 copy-start.1
  284.8 2.3 copy-start.2
Sparse Core Ops, SparseCore 0:
  19.5 41.0 all-gather.5
  63.3 38.8 all-gather.7
  104.3 38.8 all-gather.3
  146.6 66.3 reduce-scatter.6
  216.4 66.7 reduce-scatter.8
  286.5 66.8 reduce-scatter.4
  355.9 23.9 reduce-scatter.10
where the time goes:
time: 389 us
  waiting for transfers between devices  336 us (86%)
  between operations  20.3 us (5%)
  matrix products  15.1 us (4%)
  blocking collectives  8.83 us (2%)
  local copies, waits for them, and re-layouts  6.48 us (2%)
    reduce_scatter x3, waiting for transfers between devices, score_group(): lax.psum_scatter(grad_keys, 'dev', scatter_dimension=0, tiled=True)  195 us
    all_gather x3, waiting for transfers between devices, score_group(): piece = lax.all_gather(key_shard, 'dev', axis=0, tiled=True)  113 us
    reduce_scatter x1, waiting for transfers between devices, shards(): back = lax.psum_scatter(returned, 'grp', scatter_dimension=0, tiled=True)  26.6 us
    all_gather x1, blocking collectives, shards(): gathered = lax.all_gather(views_b, 'grp', axis=0, tiled=True)  8.83 us
  transfers between devices with their start and end apart: 7, of which 7 were waited for; matrix products, arithmetic and copies ran while one was open for 5% of the time, Pallas kernels for 0%

commit v1 on v0

v1 whole, which is shorter than its diff:
```python
import functools
import math

import jax
import jax.numpy as jnp
from jax import lax
from jax.experimental import pallas as pl
from jax.experimental.pallas import tpu as pltpu
from jax.sharding import PartitionSpec as P

logit_scale = 2.0
logit_bias = -6.0

MESH = pl.DeviceIdType.MESH
RIGHT, LEFT, CROSS, SIBLING = range(4)
EXTRA = 16


def dot_rows(left, right):
    return lax.dot_general(left, right, (((1,), (1,)), ((), ())), preferred_element_type=jnp.float32)


def kernel(
    n, factor, a_in, b_in, labels_in, plan, out_a, out_b,
    held_a, held_b, scaled_a, scaled_b, offsets, recv_a, recv_b, send_a, send_b,
):
    rows, width = a_in.shape
    half = n // 2
    group, member = lax.axis_index("grp"), lax.axis_index("dev")
    x, core = lax.div(group, 2), lax.rem(group, 2)
    groups = (group, (1 - x) * 2 + core, x * 2 + 1 - core, (1 - x) * 2 + 1 - core)

    odd, pair = lax.rem(member, 2), lax.div(member, 2)
    place = (1 - odd) * pair + odd * (n - 1 - pair)

    def member_at(spot):
        back = lax.div(spot, half)
        return (1 - back) * 2 * spot + back * (2 * (n - 1 - spot) + 1)

    targets = (
        (group, member_at(lax.rem(place + 1, n))),
        (group, member_at(lax.rem(place + n - 1, n))),
        (groups[1], member),
        (groups[2], member),
    )

    def behind(step):
        return lax.rem(place + n - step, n)

    def ahead(step):
        return lax.rem(place + step, n)

    def copy(side, q, spot, kind):
        held, recv, send = ((held_a, recv_a, send_a), (held_b, recv_b, send_b))[side]
        slot = groups[q] * n + spot
        return pltpu.make_async_remote_copy(
            src_ref=held.at[slot],
            dst_ref=held.at[slot],
            send_sem=send.at[kind, (q % 2) * n + spot],
            recv_sem=recv.at[slot],
            device_id=targets[kind],
            device_id_type=MESH,
        )

    def arrived(side, q, spot):
        copy(side, q, spot, SIBLING).wait_recv()

    def start(side, q, spot, kind):
        copy(side, q, spot, kind).start()

    def sent(side, q, spot, kind):
        copy(side, q, spot, kind).wait_send()

    def send_b_behind(step, act, first=None):
        @pl.when(step < half)
        def _():
            spot = behind(step)
            if first is not None:
                first(1, 0, spot)

            @pl.when(step < half - 1)
            def _():
                act(1, 0, spot, RIGHT)

            act(1, 0, spot, CROSS)
            act(1, 0, spot, SIBLING)

    def send_b_ahead(step, act, first=None):
        @pl.when(step <= half)
        def _():
            spot = ahead(step)
            if first is not None:
                first(1, 0, spot)

            @pl.when(step < half)
            def _():
                act(1, 0, spot, LEFT)

            act(1, 0, spot, CROSS)
            act(1, 0, spot, SIBLING)

    def send_a_behind(q, step, act, first=None):
        @pl.when(step <= half)
        def _():
            spot = behind(step)
            if first is not None:
                first(0, q, spot)

            @pl.when(step < half)
            def _():
                act(0, q, spot, RIGHT)

            act(0, q, spot, SIBLING)

    def send_a_ahead(q, step, act, first=None):
        @pl.when(step < half)
        def _():
            spot = ahead(step)
            if first is not None:
                first(0, q, spot)

            @pl.when(step < half - 1)
            def _():
                act(0, q, spot, LEFT)

            act(0, q, spot, SIBLING)

    def send_own(act):
        act(0, 0, place, CROSS)
        act(0, 0, place, RIGHT)
        act(1, 0, place, LEFT)
        if half > 1:
            act(1, 0, place, RIGHT)
            act(0, 0, place, LEFT)
        act(1, 0, place, CROSS)
        act(0, 0, place, SIBLING)
        act(1, 0, place, SIBLING)

    def send_crossed(act):
        act(0, 1, place, RIGHT)
        if half > 1:
            act(0, 1, place, LEFT)
        act(0, 1, place, SIBLING)

    barrier = pltpu.get_barrier_semaphore()
    for target in targets:
        pl.semaphore_signal(barrier, inc=1, device_id=target, device_id_type=MESH)

    mine = group * n + place
    labels = labels_in[...]
    high = lax.shift_right_logical(labels, 8).astype(jnp.float32)
    low = jnp.bitwise_and(labels, 255).astype(jnp.float32)
    line = lax.broadcasted_iota(jnp.int32, (EXTRA, rows), 0)
    coded = jnp.where(line == 0, high, jnp.where(line == 1, low, 0.0))
    held_a[mine, 0:rows, :] = a_in[...]
    held_a[mine, rows : rows + EXTRA, :] = coded.astype(jnp.bfloat16)
    held_b[mine] = b_in[...]
    pl.semaphore_wait(barrier, 4)
    send_own(start)

    scaled_a[...] = (a_in[...].astype(jnp.float32) * (0.5 * factor)).astype(jnp.bfloat16)
    scaled_b[...] = (b_in[...].astype(jnp.float32) * (0.5 * factor)).astype(jnp.bfloat16)
    column = lax.broadcasted_iota(jnp.int32, (rows, rows), 1).astype(jnp.float32)
    offsets[...] = (
        jnp.transpose(jnp.broadcast_to(labels.astype(jnp.float32), (rows, rows))) - column
    )
    out_a[...] = jnp.zeros_like(out_a)
    out_b[...] = jnp.zeros_like(out_b)
    own_first = ((group * n + member) * rows).astype(jnp.float32)

    arrived(0, 1, place)
    send_crossed(start)

    def bias_of(other):
        inside = other == group
        for slot in range(plan.shape[0]):
            inside = jnp.logical_or(inside, other == plan[slot, group])
        return jnp.where(inside, 0.5 * logit_bias, -1e30).astype(jnp.float32)

    def work(q, spot):
        slot = groups[q] * n + spot
        bias = bias_of(groups[q])
        first = (((groups[q] * n) + member_at(spot)) * rows).astype(jnp.float32)
        keys = held_b[slot]
        queries = held_a[slot, 0:rows, :]
        code = held_a[slot, rows : rows + EXTRA, :].astype(jnp.float32)
        found = code[0:1] * 256.0 + code[1:2] - own_first
        half_a = jnp.tanh(dot_rows(scaled_a[...], keys) + bias)
        weights = 0.5 * half_a + jnp.where(offsets[...] == first, -0.5, 0.5)
        out_a[...] += jnp.dot(
            weights.astype(jnp.bfloat16), keys, preferred_element_type=jnp.float32
        )
        half_b = jnp.tanh(dot_rows(scaled_b[...], queries) + bias)
        row = lax.broadcasted_iota(jnp.int32, (rows, rows), 0).astype(jnp.float32)
        weights = 0.5 * half_b + jnp.where(found == row, -0.5, 0.5)
        out_b[...] += jnp.dot(
            weights.astype(jnp.bfloat16), queries, preferred_element_type=jnp.float32
        )

    def step_body(step, carry):
        last = step - 1
        count = jnp.where(jnp.logical_or(last == 0, last == half), 1, 2)

        def spot_of(index):
            return lax.rem(place + n + (2 * index - 1) * last, n)

        def work_on(q):
            def body(index, carry):
                work(q, spot_of(index))
                return carry

            lax.fori_loop(0, count, body, 0)

        def receive(q):
            def body(index, carry):
                spot = spot_of(index)
                if q != 1:
                    arrived(0, q, spot)
                arrived(1, q, spot)
                if q == 1:
                    start(1, 1, spot, SIBLING)
                return carry

            lax.fori_loop(0, count, body, 0)

        work_on(0)
        receive(1)
        work_on(1)
        receive(2)
        work_on(2)
        send_b_behind(step, start, arrived)
        send_b_ahead(step, start, arrived)
        receive(3)
        work_on(3)
        for q in range(2):
            send_a_behind(q, step, start, arrived)
            send_a_ahead(q, step, start, arrived)
        return carry

    lax.fori_loop(1, half + 2, step_body, 0)

    out_a[...] = out_a[...] * factor
    out_b[...] = out_b[...] * factor

    send_own(sent)
    send_crossed(sent)

    def drain_body(step, carry):
        send_b_behind(step, sent)
        send_b_ahead(step, sent)
        for q in range(2):
            send_a_behind(q, step, sent)
            send_a_ahead(q, step, sent)
        return carry

    lax.fori_loop(1, half + 1, drain_body, 0)

    def drain_crossed(spot, carry):
        sent(1, 1, spot, SIBLING)
        return carry

    lax.fori_loop(0, n, drain_crossed, 0)


def shards(views_a, views_b, positives, plan):
    rows, width = views_a.shape
    n = lax.axis_size("dev")
    slots = lax.axis_size("grp") * n
    factor = logit_scale / math.sqrt(width)
    held = slots * (2 * rows + EXTRA) * width * 2
    vmem = pl.BlockSpec(memory_space=pltpu.VMEM)
    out = jax.ShapeDtypeStruct((rows, width), jnp.float32)
    return pl.pallas_call(
        functools.partial(kernel, n, factor),
        out_shape=(out, out),
        in_specs=[vmem, vmem, vmem, pl.BlockSpec(memory_space=pltpu.SMEM)],
        out_specs=(vmem, vmem),
        scratch_shapes=[
            pltpu.VMEM((slots, rows + EXTRA, width), jnp.bfloat16),
            pltpu.VMEM((slots, rows, width), jnp.bfloat16),
            pltpu.VMEM((rows, width), jnp.bfloat16),
            pltpu.VMEM((rows, width), jnp.bfloat16),
            pltpu.VMEM((rows, rows), jnp.float32),
            pltpu.SemaphoreType.DMA((slots,)),
            pltpu.SemaphoreType.DMA((slots,)),
            pltpu.SemaphoreType.DMA((4, slots // 2)),
            pltpu.SemaphoreType.DMA((4, slots // 2)),
        ],
        compiler_params=pltpu.CompilerParams(
            collective_id=0, has_side_effects=True, vmem_limit_bytes=held + (10 << 20)
        ),
        cost_estimate=pl.CostEstimate(
            flops=8 * slots * rows * rows * width,
            bytes_accessed=4 * rows * width * 4,
            transcendentals=2 * slots * rows * rows,
        ),
    )(views_a, views_b, positives.reshape(1, rows), plan)


def solution(mesh):
    placed = (P(("grp", "dev"), None), P(("grp", "dev"), None), P(("grp", "dev")), P())
    return jax.shard_map(
        shards,
        mesh=mesh,
        in_specs=placed,
        out_specs=(P(("grp", "dev"), None), P(("grp", "dev"), None)),
        check_vma=False,
    )
```

time: 389 us -> 50.3 us (0.13)
  waiting for transfers between devices: 336 us -> 0 us
  Pallas kernels: 0 us -> 44.9 us
  between operations: 20.3 us -> 0.65 us
  matrix products: 15.1 us -> 0 us
  blocking collectives: 8.83 us -> 0 us
    reduce_scatter x4 -> x0, waiting for transfers between devices: 221 us -> none  [the longest x3 195 us: score_group(): lax.psum_scatter(grad_keys, 'dev', scatter_dimension=0, tiled=True)]
    all_gather x3 -> x0, waiting for transfers between devices: 113 us -> none  [score_group(): piece = lax.all_gather(key_shard, 'dev', axis=0, tiled=True)]
    pallas_call x0 -> x1, Pallas kernels: none -> 44.9 us  [shards(): pl.pallas_call(functools.partial(kernel, n, factor), out_shape=(out, out)...]
    dot_general x9 -> x0, matrix products: 15.1 us -> none  [the longest x3 6.28 us: weights_for(): lax.dot_general(queries, keys, (((1,), (1,)), ((), ())), preferred_elemen...]
    all_gather x1 -> x0, blocking collectives: 8.83 us -> none  [shards(): gathered = lax.all_gather(views_b, 'grp', axis=0, tiled=True)]
    unnamed x8 -> x10, local copies, waits for them, and re-layouts: 0.02 us -> 4.57 us
  transfers between devices with their start and end apart: 7 -> 0, of which waited for: 7 -> 0; matrix products, arithmetic and copies ran while one was open for 5% -> 0% of each run, Pallas kernels for 0% -> 0%
where the time goes in v1:
time: 50.3 us; the launch traced here: 50.1 us
  Pallas kernels  44.9 us (89%)
  local copies, waits for them, and re-layouts  4.57 us (9%)
  between operations  0.65 us (1%)
    pallas_call x1, Pallas kernels, shards(): pl.pallas_call(functools.partial(kernel, n, factor), out_shape=(out, out)...  44.9 us
    unnamed x10, local copies, waits for them, and re-layouts  4.57 us

profile of v1, /device:TPU:0, one launch (start us, length us, event | category | flops | bytes accessed | tf_op | source)
XLA Modules:
  0.0 50.1 jit_solution(8469673365240919808)
XLA Ops:
  0.6 0.0 copy-start.2
  0.6 0.7 %copy-done.2 = s32[256]{0:T(256)S(1)} copy-done((s32[256]{0:T(256)S(1)}, s32[256]{0:T(256)}, u32[]{:S(2)}) %copy-start.2) | copy-done | bytes 1048
  1.3 0.0 copy-start
  1.3 0.9 %copy-done = bf16[256,256]{1,0:T(8,128)(2,1)S(1)} copy-done((bf16[256,256]{1,0:T(8,128)(2,1)S(1)}, bf16[256,256]{1,0:T(8,128)(2,1)}, u32[]{:S(2)}) %copy-start) | copy-done | bytes 131096
  2.2 0.0 copy-start.1
  2.2 0.9 %copy-done.1 = bf16[256,256]{1,0:T(8,128)(2,1)S(1)} copy-done((bf16[256,256]{1,0:T(8,128)(2,1)S(1)}, bf16[256,256]{1,0:T(8,128)(2,1)}, u32[]{:S(2)}) %copy-start.1) | copy-done | bytes 131096
  3.1 0.0 copy-start.3
  3.1 0.7 %copy-done.3 = s32[2,4]{1,0:T(2,128)S(1)} copy-done((s32[2,4]{1,0:T(2,128)S(1)}, s32[2,4]{1,0:T(2,128)}, u32[]{:S(2)}) %copy-start.3) | copy-done | bytes 56
  3.8 44.9 %shard_map.59 = (f32[256,256]{1,0:T(8,128)S(1)}, f32[256,256]{1,0:T(8,128)S(1)}) custom-call(bf16[256,256]{1,0:T(8,128)(2,1)S(1)} %copy-done, bf16[256,256]{1,0:T(8,128)(2,1)S(1)} %copy-done.1, s32[1,256]{1,0:T(1,128)S(1)} %bitcast.1, s32[2,4]{1,0:T(2,128)S(1)} %copy-done.3), custom_call_target="tpu_custom_call" | custom-call | flops 4294967296 | bytes 1048576 | tf_op jit(solution)/shard_map/pallas_call | solution.py:273
  48.7 0.7 %copy.8 = f32[256,256]{1,0:T(8,128)} copy(f32[256,256]{1,0:T(8,128)S(1)} %get-tuple-element.4) | data formatting | bytes 524288
  49.4 0.7 %copy.9 = f32[256,256]{1,0:T(8,128)} copy(f32[256,256]{1,0:T(8,128)S(1)} %get-tuple-element.5) | data formatting | bytes 524288
Async XLA Ops:
  0.6 0.7 %copy-start.2 = (s32[256]{0:T(256)S(1)}, s32[256]{0:T(256)}, u32[]{:S(2)}) copy-start(s32[256]{0:T(256)} %param.6) | copy-start | bytes 3076
  1.3 0.9 %copy-start = (bf16[256,256]{1,0:T(8,128)(2,1)S(1)}, bf16[256,256]{1,0:T(8,128)(2,1)}, u32[]{:S(2)}) copy-start(bf16[256,256]{1,0:T(8,128)(2,1)} %a_in.1) | copy-start | bytes 393220
  2.2 0.9 %copy-start.1 = (bf16[256,256]{1,0:T(8,128)(2,1)S(1)}, bf16[256,256]{1,0:T(8,128)(2,1)}, u32[]{:S(2)}) copy-start(bf16[256,256]{1,0:T(8,128)(2,1)} %b_in.1) | copy-start | bytes 393220
  3.1 0.7 %copy-start.3 = (s32[2,4]{1,0:T(2,128)S(1)}, s32[2,4]{1,0:T(2,128)}, u32[]{:S(2)}) copy-start(s32[2,4]{1,0:T(2,128)} %plan.1) | copy-start | bytes 100

commit v2 on v1

--- a/solution.py
+++ b/solution.py
@@ -21,8 +21,9 @@
 
 
 def kernel(
-    n, factor, a_in, b_in, labels_in, plan, out_a, out_b,
-    held_a, held_b, scaled_a, scaled_b, offsets, recv_a, recv_b, send_a, send_b,
+    n, factor, a_in, b_in, labels_in, plan_in, out_a, out_b,
+    held_a, held_b, scaled_a, scaled_b, offsets, labels_held, plan,
+    own_sems, recv_a, recv_b, send_a, send_b,
 ):
     rows, width = a_in.shape
     half = n // 2
@@ -100,15 +101,23 @@
             act(1, 0, spot, SIBLING)
 
     def send_a_behind(q, step, act, first=None):
-        @pl.when(step <= half)
+        farthest = half - q
+
+        @pl.when(step <= farthest)
         def _():
             spot = behind(step)
             if first is not None:
                 first(0, q, spot)
 
-            @pl.when(step < half)
+            @pl.when(step < farthest)
             def _():
                 act(0, q, spot, RIGHT)
+
+            if q == 0:
+
+                @pl.when(step == half)
+                def _():
+                    act(0, q, spot, CROSS)
 
             act(0, q, spot, SIBLING)
 
@@ -137,8 +146,8 @@
         act(1, 0, place, SIBLING)
 
     def send_crossed(act):
-        act(0, 1, place, RIGHT)
         if half > 1:
+            act(0, 1, place, RIGHT)
             act(0, 1, place, LEFT)
         act(0, 1, place, SIBLING)
 
@@ -147,19 +156,28 @@
         pl.semaphore_signal(barrier, inc=1, device_id=target, device_id_type=MESH)
 
     mine = group * n + place
-    labels = labels_in[...]
+    loads = (
+        pltpu.make_async_copy(a_in, held_a.at[mine, 0:rows, :], own_sems.at[0]),
+        pltpu.make_async_copy(b_in, held_b.at[mine], own_sems.at[1]),
+        pltpu.make_async_copy(labels_in, labels_held, own_sems.at[2]),
+        pltpu.make_async_copy(plan_in, plan, own_sems.at[3]),
+    )
+    for load in loads:
+        load.start()
+    for load in loads:
+        load.wait()
+    labels = labels_held[...]
     high = lax.shift_right_logical(labels, 8).astype(jnp.float32)
     low = jnp.bitwise_and(labels, 255).astype(jnp.float32)
     line = lax.broadcasted_iota(jnp.int32, (EXTRA, rows), 0)
     coded = jnp.where(line == 0, high, jnp.where(line == 1, low, 0.0))
-    held_a[mine, 0:rows, :] = a_in[...]
     held_a[mine, rows : rows + EXTRA, :] = coded.astype(jnp.bfloat16)
-    held_b[mine] = b_in[...]
     pl.semaphore_wait(barrier, 4)
     send_own(start)
 
-    scaled_a[...] = (a_in[...].astype(jnp.float32) * (0.5 * factor)).astype(jnp.bfloat16)
-    scaled_b[...] = (b_in[...].astype(jnp.float32) * (0.5 * factor)).astype(jnp.bfloat16)
+    own_a, own_b = held_a[mine, 0:rows, :], held_b[mine]
+    scaled_a[...] = (own_a.astype(jnp.float32) * (0.5 * factor)).astype(jnp.bfloat16)
+    scaled_b[...] = (own_b.astype(jnp.float32) * (0.5 * factor)).astype(jnp.bfloat16)
     column = lax.broadcasted_iota(jnp.int32, (rows, rows), 1).astype(jnp.float32)
     offsets[...] = (
         jnp.transpose(jnp.broadcast_to(labels.astype(jnp.float32), (rows, rows))) - column
@@ -214,7 +232,14 @@
         def receive(q):
             def body(index, carry):
                 spot = spot_of(index)
-                if q != 1:
+                if q == 1:
+
+                    @pl.when(last == half)
+                    def _():
+                        arrived(0, 1, spot)
+                        start(0, 1, spot, SIBLING)
+
+                else:
                     arrived(0, q, spot)
                 arrived(1, q, spot)
                 if q == 1:
@@ -223,18 +248,19 @@
 
             lax.fori_loop(0, count, body, 0)
 
+        send_b_behind(step, start, arrived)
+        send_b_ahead(step, start, arrived)
+        receive(1)
         work_on(0)
-        receive(1)
-        work_on(1)
+        send_a_behind(0, step, start, arrived)
+        send_a_ahead(0, step, start, arrived)
         receive(2)
         work_on(2)
-        send_b_behind(step, start, arrived)
-        send_b_ahead(step, start, arrived)
+        send_a_behind(1, step, start, arrived)
+        send_a_ahead(1, step, start, arrived)
+        work_on(1)
         receive(3)
         work_on(3)
-        for q in range(2):
-            send_a_behind(q, step, start, arrived)
-            send_a_ahead(q, step, start, arrived)
         return carry
 
     lax.fori_loop(1, half + 2, step_body, 0)
@@ -260,6 +286,7 @@
         return carry
 
     lax.fori_loop(0, n, drain_crossed, 0)
+    sent(0, 1, ahead(half), SIBLING)
 
 
 def shards(views_a, views_b, positives, plan):
@@ -273,7 +300,7 @@
     return pl.pallas_call(
         functools.partial(kernel, n, factor),
         out_shape=(out, out),
-        in_specs=[vmem, vmem, vmem, pl.BlockSpec(memory_space=pltpu.SMEM)],
+        in_specs=[pl.BlockSpec(memory_space=pltpu.HBM)] * 4,
         out_specs=(vmem, vmem),
         scratch_shapes=[
             pltpu.VMEM((slots, rows + EXTRA, width), jnp.bfloat16),
@@ -281,13 +308,16 @@
             pltpu.VMEM((rows, width), jnp.bfloat16),
             pltpu.VMEM((rows, width), jnp.bfloat16),
             pltpu.VMEM((rows, rows), jnp.float32),
+            pltpu.VMEM((1, rows), jnp.int32),
+            pltpu.SMEM(plan.shape, jnp.int32),
+            pltpu.SemaphoreType.DMA((4,)),
             pltpu.SemaphoreType.DMA((slots,)),
             pltpu.SemaphoreType.DMA((slots,)),
             pltpu.SemaphoreType.DMA((4, slots // 2)),
             pltpu.SemaphoreType.DMA((4, slots // 2)),
         ],
         compiler_params=pltpu.CompilerParams(
-            collective_id=0, has_side_effects=True, vmem_limit_bytes=held + (10 << 20)
+            collective_id=0, has_side_effects=True, vmem_limit_bytes=60 << 20
         ),
         cost_estimate=pl.CostEstimate(
             flops=8 * slots * rows * rows * width,

time: 50.3 us -> 49.7 us (0.988)
  local copies, waits for them, and re-layouts: 4.57 us -> 2.42 us
  Pallas kernels: 44.9 us -> 46.5 us
    unnamed x10 -> x4, local copies, waits for them, and re-layouts: 4.57 us -> 2.42 us
    pallas_call x1, Pallas kernels: 44.9 us -> 46.5 us  [shards(): pl.pallas_call(functools.partial(kernel, n, factor), out_shape=(out, out)...]
where the time goes in v2:
time: 49.7 us; the launch traced here: 49.6 us
  Pallas kernels  46.5 us (94%)
  local copies, waits for them, and re-layouts  2.42 us (5%)
  between operations  0.65 us (1%)
    pallas_call x1, Pallas kernels, shards(): pl.pallas_call(functools.partial(kernel, n, factor), out_shape=(out, out)...  46.5 us
    unnamed x4, local copies, waits for them, and re-layouts  2.42 us

profile of v2, /device:TPU:0, one launch (start us, length us, event | category | flops | bytes accessed | tf_op | source)
XLA Modules:
  0.0 49.6 jit_solution(185144446437034903)
XLA Ops:
  0.6 46.5 %shard_map.59 = (f32[256,256]{1,0:T(8,128)}, f32[256,256]{1,0:T(8,128)}) custom-call(bf16[256,256]{1,0:T(8,128)(2,1)} %a_in.1, bf16[256,256]{1,0:T(8,128)(2,1)} %b_in.1, s32[1,256]{1,0:T(1,128)} %bitcast.1, s32[2,4]{1,0:T(2,128)} %plan_in.1), custom_call_target="tpu_custom_call" | custom-call | flops 4294967296 | bytes 1048576 | tf_op jit(solution)/shard_map/pallas_call | solution.py:300
  47.1 0.0 copy-start
  47.2 1.7 %copy.8 = f32[256,256]{1,0:T(8,128)} copy(f32[256,256]{1,0:T(8,128)} %get-tuple-element.4) | data formatting | bytes 524288
  48.9 0.0 copy-done
  48.9 0.7 %copy.9 = f32[256,256]{1,0:T(8,128)} copy(f32[256,256]{1,0:T(8,128)S(1)} %copy-done) | data formatting | bytes 524288
Async XLA Ops:
  47.1 1.7 %copy-start = (f32[256,256]{1,0:T(8,128)S(1)}, f32[256,256]{1,0:T(8,128)}, u32[]{:S(2)}) copy-start(f32[256,256]{1,0:T(8,128)} %get-tuple-element.5) | copy-start | bytes 786436

commit v3 on v2

--- a/solution.py
+++ b/solution.py
@@ -53,7 +53,7 @@
 
     def copy(side, q, spot, kind):
         held, recv, send = ((held_a, recv_a, send_a), (held_b, recv_b, send_b))[side]
-        slot = groups[q] * n + spot
+        slot = spot * 4 + groups[q]
         return pltpu.make_async_remote_copy(
             src_ref=held.at[slot],
             dst_ref=held.at[slot],
@@ -155,7 +155,7 @@
     for target in targets:
         pl.semaphore_signal(barrier, inc=1, device_id=target, device_id_type=MESH)
 
-    mine = group * n + place
+    mine = place * 4 + group
     loads = (
         pltpu.make_async_copy(a_in, held_a.at[mine, 0:rows, :], own_sems.at[0]),
         pltpu.make_async_copy(b_in, held_b.at[mine], own_sems.at[1]),
@@ -195,24 +195,34 @@
             inside = jnp.logical_or(inside, other == plan[slot, group])
         return jnp.where(inside, 0.5 * logit_bias, -1e30).astype(jnp.float32)
 
-    def work(q, spot):
-        slot = groups[q] * n + spot
-        bias = bias_of(groups[q])
-        first = (((groups[q] * n) + member_at(spot)) * rows).astype(jnp.float32)
-        keys = held_b[slot]
-        queries = held_a[slot, 0:rows, :]
-        code = held_a[slot, rows : rows + EXTRA, :].astype(jnp.float32)
-        found = code[0:1] * 256.0 + code[1:2] - own_first
-        half_a = jnp.tanh(dot_rows(scaled_a[...], keys) + bias)
-        weights = 0.5 * half_a + jnp.where(offsets[...] == first, -0.5, 0.5)
+    biases = [bias_of(other) for other in range(4)]
+
+    def work(spot):
+        base = spot * 4
+        at = member_at(spot) * rows
+        row = lax.broadcasted_iota(jnp.int32, (rows, rows), 0).astype(jnp.float32)
+        keys, queries, key_weights, query_weights = [], [], [], []
+        for other in range(4):
+            first = (other * n * rows + at).astype(jnp.float32)
+            keys.append(held_b[base + other])
+            queries.append(held_a[base + other, 0:rows, :])
+            code = held_a[base + other, rows : rows + EXTRA, :].astype(jnp.float32)
+            found = code[0:1] * 256.0 + code[1:2] - own_first
+            twice = jnp.tanh(dot_rows(scaled_a[...], keys[-1]) + biases[other])
+            twice += jnp.where(offsets[...] == first, -1.0, 1.0)
+            key_weights.append(twice.astype(jnp.bfloat16))
+            twice = jnp.tanh(dot_rows(scaled_b[...], queries[-1]) + biases[other])
+            twice += jnp.where(found == row, -1.0, 1.0)
+            query_weights.append(twice.astype(jnp.bfloat16))
         out_a[...] += jnp.dot(
-            weights.astype(jnp.bfloat16), keys, preferred_element_type=jnp.float32
+            jnp.concatenate(key_weights, 1),
+            jnp.concatenate(keys, 0),
+            preferred_element_type=jnp.float32,
         )
-        half_b = jnp.tanh(dot_rows(scaled_b[...], queries) + bias)
-        row = lax.broadcasted_iota(jnp.int32, (rows, rows), 0).astype(jnp.float32)
-        weights = 0.5 * half_b + jnp.where(found == row, -0.5, 0.5)
         out_b[...] += jnp.dot(
-            weights.astype(jnp.bfloat16), queries, preferred_element_type=jnp.float32
+            jnp.concatenate(query_weights, 1),
+            jnp.concatenate(queries, 0),
+            preferred_element_type=jnp.float32,
         )
 
     def step_body(step, carry):
@@ -222,51 +232,43 @@
         def spot_of(index):
             return lax.rem(place + n + (2 * index - 1) * last, n)
 
-        def work_on(q):
-            def body(index, carry):
-                work(q, spot_of(index))
-                return carry
-
-            lax.fori_loop(0, count, body, 0)
-
-        def receive(q):
-            def body(index, carry):
-                spot = spot_of(index)
-                if q == 1:
-
-                    @pl.when(last == half)
-                    def _():
-                        arrived(0, 1, spot)
-                        start(0, 1, spot, SIBLING)
-
-                else:
-                    arrived(0, q, spot)
-                arrived(1, q, spot)
-                if q == 1:
-                    start(1, 1, spot, SIBLING)
-                return carry
-
-            lax.fori_loop(0, count, body, 0)
+        def receive(q, spot):
+            if q == 1:
+
+                @pl.when(last == half)
+                def _():
+                    arrived(0, 1, spot)
+                    start(0, 1, spot, SIBLING)
+
+            else:
+                arrived(0, q, spot)
+            arrived(1, q, spot)
+            if q == 1:
+                start(1, 1, spot, SIBLING)
+
+        def turn(index, carry):
+            spot = spot_of(index)
+            for q in (1, 2, 3):
+                receive(q, spot)
+            work(spot)
+
+            @pl.when(index == 0)
+            def _():
+                for q in range(2):
+                    send_a_behind(q, step, start, arrived)
+                    send_a_ahead(q, step, start, arrived)
+
+            return carry
 
         send_b_behind(step, start, arrived)
         send_b_ahead(step, start, arrived)
-        receive(1)
-        work_on(0)
-        send_a_behind(0, step, start, arrived)
-        send_a_ahead(0, step, start, arrived)
-        receive(2)
-        work_on(2)
-        send_a_behind(1, step, start, arrived)
-        send_a_ahead(1, step, start, arrived)
-        work_on(1)
-        receive(3)
-        work_on(3)
+        lax.fori_loop(0, count, turn, 0)
         return carry
 
     lax.fori_loop(1, half + 2, step_body, 0)
 
-    out_a[...] = out_a[...] * factor
-    out_b[...] = out_b[...] * factor
+    out_a[...] = out_a[...] * (0.5 * factor)
+    out_b[...] = out_b[...] * (0.5 * factor)
 
     send_own(sent)
     send_crossed(sent)

time: 49.7 us -> 50.7 us (1.020)
  Pallas kernels: 46.5 us -> 47.2 us
    pallas_call x1, Pallas kernels: 46.5 us -> 47.2 us  [shards(): pl.pallas_call(functools.partial(kernel, n, factor), out_shape=(out, out)...]
where the time goes in v3:
time: 50.7 us; the launch traced here: 50.3 us
  Pallas kernels  47.2 us (93%)
  local copies, waits for them, and re-layouts  2.42 us (5%)
  between operations  0.65 us (1%)
    pallas_call x1, Pallas kernels, shards(): pl.pallas_call(functools.partial(kernel, n, factor), out_shape=(out, out)...  47.2 us
    unnamed x4, local copies, waits for them, and re-layouts  2.42 us

profile of v3, /device:TPU:0, one launch (start us, length us, event | category | flops | bytes accessed | tf_op | source)
XLA Modules:
  0.0 50.3 jit_solution(10776765107250756316)
XLA Ops:
  0.6 47.2 %shard_map.59 = (f32[256,256]{1,0:T(8,128)}, f32[256,256]{1,0:T(8,128)}) custom-call(bf16[256,256]{1,0:T(8,128)(2,1)} %a_in.1, bf16[256,256]{1,0:T(8,128)(2,1)} %b_in.1, s32[1,256]{1,0:T(1,128)} %bitcast.1, s32[2,4]{1,0:T(2,128)} %plan_in.1), custom_call_target="tpu_custom_call" | custom-call | flops 4294967296 | bytes 1048576 | tf_op jit(solution)/shard_map/pallas_call | solution.py:302
  47.9 0.0 copy-start
  47.9 1.7 %copy.8 = f32[256,256]{1,0:T(8,128)} copy(f32[256,256]{1,0:T(8,128)} %get-tuple-element.4) | data formatting | bytes 524288
  49.6 0.0 copy-done
  49.6 0.7 %copy.9 = f32[256,256]{1,0:T(8,128)} copy(f32[256,256]{1,0:T(8,128)S(1)} %copy-done) | data formatting | bytes 524288
Async XLA Ops:
  47.9 1.7 %copy-start = (f32[256,256]{1,0:T(8,128)S(1)}, f32[256,256]{1,0:T(8,128)}, u32[]{:S(2)}) copy-start(f32[256,256]{1,0:T(8,128)} %get-tuple-element.5) | copy-start | bytes 786436

commit v4 on v3

v4 whole, which is shorter than its diff:
```python
import functools
import math

import jax
import jax.numpy as jnp
from jax import lax
from jax.experimental import pallas as pl
from jax.experimental.pallas import tpu as pltpu
from jax.sharding import PartitionSpec as P

logit_scale = 2.0
logit_bias = -6.0

MESH = pl.DeviceIdType.MESH
RIGHT, LEFT, CROSS, SIBLING = range(4)
EXTRA = 16


def dot_rows(left, right):
    return lax.dot_general(left, right, (((1,), (1,)), ((), ())), preferred_element_type=jnp.float32)


def kernel(
    n, factor, a_in, b_in, labels_in, plan_in, out_a, out_b,
    held_a, held_b, mate_a, mate_b, total_a, total_b, share_a, share_b,
    scaled_a, scaled_b, offsets, labels_held, plan,
    own_sems, recv_a, recv_b, send_a, send_b, mate_send, mate_recv,
):
    rows, width = a_in.shape
    half = n // 2
    group, member = lax.axis_index("grp"), lax.axis_index("dev")
    x, core = lax.div(group, 2), lax.rem(group, 2)
    across, mate = (1 - x) * 2 + core, x * 2 + 1 - core

    odd, pair = lax.rem(member, 2), lax.div(member, 2)
    place = (1 - odd) * pair + odd * (n - 1 - pair)

    def member_at(spot):
        back = lax.div(spot, half)
        return (1 - back) * 2 * spot + back * (2 * (n - 1 - spot) + 1)

    targets = (
        (group, member_at(lax.rem(place + 1, n))),
        (group, member_at(lax.rem(place + n - 1, n))),
        (across, member),
        (mate, member),
    )

    def behind(step):
        return lax.rem(place + n - step, n)

    def ahead(step):
        return lax.rem(place + step, n)

    def copy(side, q, spot, kind):
        held, recv, send = ((held_a, recv_a, send_a), (held_b, recv_b, send_b))[side]
        slot = spot * 2 + (x if q == 0 else 1 - x)
        return pltpu.make_async_remote_copy(
            src_ref=held.at[slot],
            dst_ref=held.at[slot],
            send_sem=send.at[kind, q * n + spot],
            recv_sem=recv.at[slot],
            device_id=targets[kind],
            device_id_type=MESH,
        )

    def arrived(side, q, spot):
        copy(side, q, spot, CROSS).wait_recv()

    def start(side, q, spot, kind):
        copy(side, q, spot, kind).start()

    def sent(side, q, spot, kind):
        copy(side, q, spot, kind).wait_send()

    def send_b_behind(step, act, first=None):
        @pl.when(step < half)
        def _():
            spot = behind(step)
            if first is not None:
                first(1, 0, spot)

            @pl.when(step < half - 1)
            def _():
                act(1, 0, spot, RIGHT)

            act(1, 0, spot, CROSS)

    def send_b_ahead(step, act, first=None):
        @pl.when(step <= half)
        def _():
            spot = ahead(step)
            if first is not None:
                first(1, 0, spot)

            @pl.when(step < half)
            def _():
                act(1, 0, spot, LEFT)

            act(1, 0, spot, CROSS)

    def send_a_behind(q, step, act, first=None):
        farthest = half - q

        @pl.when(step <= farthest)
        def _():
            spot = behind(step)
            if first is not None:
                first(0, q, spot)

            @pl.when(step < farthest)
            def _():
                act(0, q, spot, RIGHT)

            if q == 0:

                @pl.when(step == half)
                def _():
                    act(0, q, spot, CROSS)

    def send_a_ahead(q, step, act, first=None):
        @pl.when(step < half)
        def _():
            spot = ahead(step)
            if first is not None:
                first(0, q, spot)

            @pl.when(step < half - 1)
            def _():
                act(0, q, spot, LEFT)

    def send_own(act):
        act(0, 0, place, CROSS)
        act(0, 0, place, RIGHT)
        act(1, 0, place, LEFT)
        if half > 1:
            act(1, 0, place, RIGHT)
            act(0, 0, place, LEFT)
        act(1, 0, place, CROSS)

    def send_crossed(act):
        if half > 1:
            act(0, 1, place, RIGHT)
            act(0, 1, place, LEFT)

    def to_mate(source, target, index):
        return pltpu.make_async_remote_copy(
            src_ref=source,
            dst_ref=target,
            send_sem=mate_send.at[index],
            recv_sem=mate_recv.at[index],
            device_id=targets[SIBLING],
            device_id_type=MESH,
        )

    barrier = pltpu.get_barrier_semaphore()
    for target in targets:
        pl.semaphore_signal(barrier, inc=1, device_id=target, device_id_type=MESH)

    mine = place * 2 + x
    loads = (
        pltpu.make_async_copy(a_in, held_a.at[mine, 0:rows, :], own_sems.at[0]),
        pltpu.make_async_copy(b_in, held_b.at[mine], own_sems.at[1]),
        pltpu.make_async_copy(labels_in, labels_held, own_sems.at[2]),
        pltpu.make_async_copy(plan_in, plan, own_sems.at[3]),
    )
    for load in loads:
        load.start()
    for load in loads:
        load.wait()
    labels = labels_held[...]
    high = lax.shift_right_logical(labels, 8).astype(jnp.float32)
    low = jnp.bitwise_and(labels, 255).astype(jnp.float32)
    line = lax.broadcasted_iota(jnp.int32, (EXTRA, rows), 0)
    coded = jnp.where(line == 0, high, jnp.where(line == 1, low, 0.0))
    held_a[mine, rows : rows + EXTRA, :] = coded.astype(jnp.bfloat16)
    pl.semaphore_wait(barrier, 4)
    send_own(start)
    own_to_mate = (
        to_mate(held_a.at[mine], mate_a, 0),
        to_mate(held_b.at[mine], mate_b, 1),
    )
    for each in own_to_mate:
        each.start()

    def decode(code):
        code = code.astype(jnp.float32)
        return code[0:1] * 256.0 + code[1:2]

    column = lax.broadcasted_iota(jnp.int32, (rows, rows), 1).astype(jnp.float32)

    def take(index, block_a, block_b, marks):
        part = slice(index * rows, (index + 1) * rows)
        scaled_a[part] = (block_a.astype(jnp.float32) * (0.5 * factor)).astype(jnp.bfloat16)
        scaled_b[part] = (block_b.astype(jnp.float32) * (0.5 * factor)).astype(jnp.bfloat16)
        offsets[part] = jnp.transpose(jnp.broadcast_to(marks, (rows, rows))) - column

    take(0, held_a[mine, 0:rows, :], held_b[mine], labels.astype(jnp.float32))
    total_a[...] = jnp.zeros_like(total_a)
    total_b[...] = jnp.zeros_like(total_b)

    arrived(0, 1, place)
    send_crossed(start)
    for each in own_to_mate:
        each.wait_recv()
    take(1, mate_a[0:rows, :], mate_b[...], decode(mate_a[rows : rows + EXTRA, :]))

    def bias_of(one, other):
        inside = other == one
        for slot in range(plan.shape[0]):
            inside = jnp.logical_or(inside, other == plan[slot, one])
        return jnp.where(inside, 0.5 * logit_bias, -1e30).astype(jnp.float32)

    owners = (group, mate)
    others = (core, 2 + core)
    biases = [[bias_of(one, other) for one in owners] for other in others]
    firsts = [((one * n + member) * rows).astype(jnp.float32) for one in owners]

    def work(spot):
        base = spot * 2
        at = member_at(spot) * rows
        row = lax.broadcasted_iota(jnp.int32, (rows, rows), 0).astype(jnp.float32)
        keys = [held_b[base + index] for index in range(2)]
        queries = [held_a[base + index, 0:rows, :] for index in range(2)]
        marks = [decode(held_a[base + index, rows : rows + EXTRA, :]) for index in range(2)]
        all_keys, all_queries = jnp.concatenate(keys, 0), jnp.concatenate(queries, 0)
        for index in range(2):
            part = slice(index * rows, (index + 1) * rows)
            key_weights, query_weights = [], []
            for other in range(2):
                bias = biases[other][index]
                first = (others[other] * n * rows + at).astype(jnp.float32)
                twice = jnp.tanh(dot_rows(scaled_a[part], keys[other]) + bias)
                twice += jnp.where(offsets[part] == first, -1.0, 1.0)
                key_weights.append(twice.astype(jnp.bfloat16))
                twice = jnp.tanh(dot_rows(scaled_b[part], queries[other]) + bias)
                twice += jnp.where(marks[other] - firsts[index] == row, -1.0, 1.0)
                query_weights.append(twice.astype(jnp.bfloat16))
            total_a[part] += jnp.dot(
                jnp.concatenate(key_weights, 1), all_keys, preferred_element_type=jnp.float32
            )
            total_b[part] += jnp.dot(
                jnp.concatenate(query_weights, 1), all_queries, preferred_element_type=jnp.float32
            )

    def step_body(step, carry):
        last = step - 1
        count = jnp.where(jnp.logical_or(last == 0, last == half), 1, 2)

        def turn(index, carry):
            spot = lax.rem(place + n + (2 * index - 1) * last, n)

            @pl.when(last == half)
            def _():
                arrived(0, 1, spot)

            arrived(1, 1, spot)
            work(spot)

            @pl.when(index == 0)
            def _():
                for q in range(2):
                    send_a_behind(q, step, start, arrived)
                    send_a_ahead(q, step, start, arrived)

            return carry

        send_b_behind(step, start, arrived)
        send_b_ahead(step, start, arrived)
        lax.fori_loop(0, count, turn, 0)
        return carry

    lax.fori_loop(1, half + 2, step_body, 0)

    shares = (
        to_mate(total_a.at[rows : 2 * rows], share_a, 2),
        to_mate(total_b.at[rows : 2 * rows], share_b, 3),
    )
    for each in shares:
        each.start()

    send_own(sent)
    send_crossed(sent)
    for each in own_to_mate:
        each.wait_send()

    def drain_body(step, carry):
        send_b_behind(step, sent)
        send_b_ahead(step, sent)
        for q in range(2):
            send_a_behind(q, step, sent)
            send_a_ahead(q, step, sent)
        return carry

    lax.fori_loop(1, half + 1, drain_body, 0)

    shares[0].wait_recv()
    out_a[...] = (total_a[0:rows] + share_a[...]) * (0.5 * factor)
    shares[1].wait_recv()
    out_b[...] = (total_b[0:rows] + share_b[...]) * (0.5 * factor)
    for each in shares:
        each.wait_send()


def shards(views_a, views_b, positives, plan):
    rows, width = views_a.shape
    n = lax.axis_size("dev")
    slots = 2 * n
    factor = logit_scale / math.sqrt(width)
    vmem = pl.BlockSpec(memory_space=pltpu.VMEM)
    out = jax.ShapeDtypeStruct((rows, width), jnp.float32)
    return pl.pallas_call(
        functools.partial(kernel, n, factor),
        out_shape=(out, out),
        in_specs=[pl.BlockSpec(memory_space=pltpu.HBM)] * 4,
        out_specs=(vmem, vmem),
        scratch_shapes=[
            pltpu.VMEM((slots, rows + EXTRA, width), jnp.bfloat16),
            pltpu.VMEM((slots, rows, width), jnp.bfloat16),
            pltpu.VMEM((rows + EXTRA, width), jnp.bfloat16),
            pltpu.VMEM((rows, width), jnp.bfloat16),
            pltpu.VMEM((2 * rows, width), jnp.float32),
            pltpu.VMEM((2 * rows, width), jnp.float32),
            pltpu.VMEM((rows, width), jnp.float32),
            pltpu.VMEM((rows, width), jnp.float32),
            pltpu.VMEM((2 * rows, width), jnp.bfloat16),
            pltpu.VMEM((2 * rows, width), jnp.bfloat16),
            pltpu.VMEM((2 * rows, rows), jnp.float32),
            pltpu.VMEM((1, rows), jnp.int32),
            pltpu.SMEM(plan.shape, jnp.int32),
            pltpu.SemaphoreType.DMA((4,)),
            pltpu.SemaphoreType.DMA((slots,)),
            pltpu.SemaphoreType.DMA((slots,)),
            pltpu.SemaphoreType.DMA((3, slots)),
            pltpu.SemaphoreType.DMA((3, slots)),
            pltpu.SemaphoreType.DMA((4,)),
            pltpu.SemaphoreType.DMA((4,)),
        ],
        compiler_params=pltpu.CompilerParams(
            collective_id=0, has_side_effects=True, vmem_limit_bytes=60 << 20
        ),
        cost_estimate=pl.CostEstimate(
            flops=16 * slots * rows * rows * width,
            bytes_accessed=4 * rows * width * 4,
            transcendentals=4 * slots * rows * rows,
        ),
    )(views_a, views_b, positives.reshape(1, rows), plan)


def solution(mesh):
    placed = (P(("grp", "dev"), None), P(("grp", "dev"), None), P(("grp", "dev")), P())
    return jax.shard_map(
        shards,
        mesh=mesh,
        in_specs=placed,
        out_specs=(P(("grp", "dev"), None), P(("grp", "dev"), None)),
        check_vma=False,
    )
```

time: 50.7 us -> 49 us (0.966)
  Pallas kernels: 47.2 us -> 45.7 us
    pallas_call x1, Pallas kernels: 47.2 us -> 45.7 us  [shards(): pl.pallas_call(functools.partial(kernel, n, factor), out_shape=(out, out)...]
where the time goes in v4:
time: 49 us; the launch traced here: 48.8 us
  Pallas kernels  45.7 us (93%)
  local copies, waits for them, and re-layouts  2.42 us (5%)
  between operations  0.65 us (1%)
    pallas_call x1, Pallas kernels, shards(): pl.pallas_call(functools.partial(kernel, n, factor), out_shape=(out, out)...  45.7 us
    unnamed x4, local copies, waits for them, and re-layouts  2.42 us

profile of v4, /device:TPU:0, one launch (start us, length us, event | category | flops | bytes accessed | tf_op | source)
XLA Modules:
  0.0 48.8 jit_solution(15629317773772543766)
XLA Ops:
  0.6 45.7 %shard_map.59 = (f32[256,256]{1,0:T(8,128)}, f32[256,256]{1,0:T(8,128)}) custom-call(bf16[256,256]{1,0:T(8,128)(2,1)} %a_in.1, bf16[256,256]{1,0:T(8,128)(2,1)} %b_in.1, s32[1,256]{1,0:T(1,128)} %bitcast.1, s32[2,4]{1,0:T(2,128)} %plan_in.1), custom_call_target="tpu_custom_call" | custom-call | flops 4294967296 | bytes 1048576 | tf_op jit(solution)/shard_map/pallas_call | solution.py:312
  46.4 0.0 copy-start
  46.4 1.7 %copy.8 = f32[256,256]{1,0:T(8,128)} copy(f32[256,256]{1,0:T(8,128)} %get-tuple-element.4) | data formatting | bytes 524288
  48.1 0.0 copy-done
  48.1 0.7 %copy.9 = f32[256,256]{1,0:T(8,128)} copy(f32[256,256]{1,0:T(8,128)S(1)} %copy-done) | data formatting | bytes 524288
Async XLA Ops:
  46.4 1.7 %copy-start = (f32[256,256]{1,0:T(8,128)S(1)}, f32[256,256]{1,0:T(8,128)}, u32[]{:S(2)}) copy-start(f32[256,256]{1,0:T(8,128)} %get-tuple-element.5) | copy-start | bytes 786436

commit v5 on v4

--- a/solution.py
+++ b/solution.py
@@ -112,36 +112,33 @@
             def _():
                 act(0, q, spot, RIGHT)
 
-            if q == 0:
-
-                @pl.when(step == half)
-                def _():
-                    act(0, q, spot, CROSS)
-
     def send_a_ahead(q, step, act, first=None):
-        @pl.when(step < half)
+        farthest = half - 1 + q
+
+        @pl.when(step <= farthest)
         def _():
             spot = ahead(step)
             if first is not None:
                 first(0, q, spot)
 
-            @pl.when(step < half - 1)
+            @pl.when(step < farthest)
             def _():
                 act(0, q, spot, LEFT)
 
     def send_own(act):
-        act(0, 0, place, CROSS)
-        act(0, 0, place, RIGHT)
         act(1, 0, place, LEFT)
         if half > 1:
             act(1, 0, place, RIGHT)
+        act(0, 0, place, CROSS)
+        act(0, 0, place, RIGHT)
+        if half > 1:
             act(0, 0, place, LEFT)
         act(1, 0, place, CROSS)
 
     def send_crossed(act):
+        act(0, 1, place, LEFT)
         if half > 1:
             act(0, 1, place, RIGHT)
-            act(0, 1, place, LEFT)
 
     def to_mate(source, target, index):
         return pltpu.make_async_remote_copy(
@@ -249,25 +246,23 @@
 
         def turn(index, carry):
             spot = lax.rem(place + n + (2 * index - 1) * last, n)
-
-            @pl.when(last == half)
-            def _():
-                arrived(0, 1, spot)
-
             arrived(1, 1, spot)
             work(spot)
 
             @pl.when(index == 0)
             def _():
-                for q in range(2):
-                    send_a_behind(q, step, start, arrived)
-                    send_a_ahead(q, step, start, arrived)
+                send_a_behind(0, step, start, arrived)
+                send_a_ahead(0, step, start, arrived)
+                send_b_behind(2 * step, start, arrived)
+                send_b_ahead(2 * step, start, arrived)
 
             return carry
 
-        send_b_behind(step, start, arrived)
-        send_b_ahead(step, start, arrived)
+        send_b_behind(2 * step - 1, start, arrived)
+        send_b_ahead(2 * step - 1, start, arrived)
         lax.fori_loop(0, count, turn, 0)
+        send_a_behind(1, step, start, arrived)
+        send_a_ahead(1, step, start, arrived)
         return carry
 
     lax.fori_loop(1, half + 2, step_body, 0)

time: 49 us -> 47.3 us (0.965)
  Pallas kernels: 45.7 us -> 44.1 us
    pallas_call x1, Pallas kernels: 45.7 us -> 44.1 us  [shards(): pl.pallas_call(functools.partial(kernel, n, factor), out_shape=(out, out)...]
where the time goes in v5:
time: 47.3 us; the launch traced here: 47.2 us
  Pallas kernels  44.1 us (93%)
  local copies, waits for them, and re-layouts  2.42 us (5%)
  between operations  0.65 us (1%)
    pallas_call x1, Pallas kernels, shards(): pl.pallas_call(functools.partial(kernel, n, factor), out_shape=(out, out)...  44.1 us
    unnamed x4, local copies, waits for them, and re-layouts  2.42 us

profile of v5, /device:TPU:0, one launch (start us, length us, event | category | flops | bytes accessed | tf_op | source)
XLA Modules:
  0.0 47.2 jit_solution(7749681353676992778)
XLA Ops:
  0.6 44.1 %shard_map.59 = (f32[256,256]{1,0:T(8,128)}, f32[256,256]{1,0:T(8,128)}) custom-call(bf16[256,256]{1,0:T(8,128)(2,1)} %a_in.1, bf16[256,256]{1,0:T(8,128)(2,1)} %b_in.1, s32[1,256]{1,0:T(1,128)} %bitcast.1, s32[2,4]{1,0:T(2,128)} %plan_in.1), custom_call_target="tpu_custom_call" | custom-call | flops 4294967296 | bytes 1048576 | tf_op jit(solution)/shard_map/pallas_call | solution.py:307
  44.8 0.0 copy-start
  44.8 1.7 %copy.8 = f32[256,256]{1,0:T(8,128)} copy(f32[256,256]{1,0:T(8,128)} %get-tuple-element.4) | data formatting | bytes 524288
  46.5 0.0 copy-done
  46.5 0.7 %copy.9 = f32[256,256]{1,0:T(8,128)} copy(f32[256,256]{1,0:T(8,128)S(1)} %copy-done) | data formatting | bytes 524288
Async XLA Ops:
  44.8 1.7 %copy-start = (f32[256,256]{1,0:T(8,128)S(1)}, f32[256,256]{1,0:T(8,128)}, u32[]{:S(2)}) copy-start(f32[256,256]{1,0:T(8,128)} %get-tuple-element.5) | copy-start | bytes 786436

commit v6 on v5

--- a/solution.py
+++ b/solution.py
@@ -186,13 +186,28 @@
 
     column = lax.broadcasted_iota(jnp.int32, (rows, rows), 1).astype(jnp.float32)
 
-    def take(index, block_a, block_b, marks):
-        part = slice(index * rows, (index + 1) * rows)
-        scaled_a[part] = (block_a.astype(jnp.float32) * (0.5 * factor)).astype(jnp.bfloat16)
-        scaled_b[part] = (block_b.astype(jnp.float32) * (0.5 * factor)).astype(jnp.bfloat16)
-        offsets[part] = jnp.transpose(jnp.broadcast_to(marks, (rows, rows))) - column
-
-    take(0, held_a[mine, 0:rows, :], held_b[mine], labels.astype(jnp.float32))
+    missing = sum(range(4)) - group
+    for slot in range(plan.shape[0]):
+        missing -= plan[slot, group]
+    swap_1 = missing == across
+    swap_2 = missing == 3 - group
+    swaps = (None, swap_1, swap_2)
+
+    def pick(swap, one, other):
+        return lax.select(jnp.broadcast_to(swap, one.shape), one, other)
+
+    def scale(block):
+        return (block.astype(jnp.float32) * (0.5 * factor)).astype(jnp.bfloat16)
+
+    def spread(marks):
+        return jnp.transpose(jnp.broadcast_to(marks, (rows, rows))) - column
+
+    def part_of(index):
+        return slice(index * rows, (index + 1) * rows)
+
+    scaled_a[part_of(0)] = scale(held_a[mine, 0:rows, :])
+    scaled_b[part_of(0)] = scale(held_b[mine])
+    offsets[part_of(0)] = spread(labels.astype(jnp.float32))
     total_a[...] = jnp.zeros_like(total_a)
     total_b[...] = jnp.zeros_like(total_b)
 
@@ -200,44 +215,42 @@
     send_crossed(start)
     for each in own_to_mate:
         each.wait_recv()
-    take(1, mate_a[0:rows, :], mate_b[...], decode(mate_a[rows : rows + EXTRA, :]))
-
-    def bias_of(one, other):
-        inside = other == one
-        for slot in range(plan.shape[0]):
-            inside = jnp.logical_or(inside, other == plan[slot, one])
-        return jnp.where(inside, 0.5 * logit_bias, -1e30).astype(jnp.float32)
-
-    owners = (group, mate)
-    others = (core, 2 + core)
-    biases = [[bias_of(one, other) for one in owners] for other in others]
-    firsts = [((one * n + member) * rows).astype(jnp.float32) for one in owners]
+    scaled_a[part_of(2)] = scale(mate_a[0:rows, :])
+    scaled_b[part_of(2)] = scale(mate_b[...])
+    offsets[part_of(2)] = spread(decode(mate_a[rows : rows + EXTRA, :]))
+    for ref in (scaled_a, scaled_b, offsets):
+        ref[part_of(1)] = pick(swap_1, ref[part_of(2)], ref[part_of(0)])
+
+    owners = (group, jnp.where(swap_1, mate, group), mate)
+    others = (group, jnp.where(swap_1, group, across), jnp.where(swap_2, group, across))
+    own_firsts = [((one * n + member) * rows).astype(jnp.float32) for one in owners]
 
     def work(spot):
         base = spot * 2
         at = member_at(spot) * rows
         row = lax.broadcasted_iota(jnp.int32, (rows, rows), 0).astype(jnp.float32)
-        keys = [held_b[base + index] for index in range(2)]
-        queries = [held_a[base + index, 0:rows, :] for index in range(2)]
-        marks = [decode(held_a[base + index, rows : rows + EXTRA, :]) for index in range(2)]
-        all_keys, all_queries = jnp.concatenate(keys, 0), jnp.concatenate(queries, 0)
-        for index in range(2):
-            part = slice(index * rows, (index + 1) * rows)
-            key_weights, query_weights = [], []
-            for other in range(2):
-                bias = biases[other][index]
-                first = (others[other] * n * rows + at).astype(jnp.float32)
-                twice = jnp.tanh(dot_rows(scaled_a[part], keys[other]) + bias)
-                twice += jnp.where(offsets[part] == first, -1.0, 1.0)
-                key_weights.append(twice.astype(jnp.bfloat16))
-                twice = jnp.tanh(dot_rows(scaled_b[part], queries[other]) + bias)
-                twice += jnp.where(marks[other] - firsts[index] == row, -1.0, 1.0)
-                query_weights.append(twice.astype(jnp.bfloat16))
+        near, far = base + x, base + 1 - x
+        near_keys, far_keys = held_b[near], held_b[far]
+        near_queries, far_queries = held_a[near, 0:rows, :], held_a[far, 0:rows, :]
+        near_marks = decode(held_a[near, rows : rows + EXTRA, :])
+        far_marks = decode(held_a[far, rows : rows + EXTRA, :])
+        for index in range(3):
+            part = part_of(index)
+            keys, queries, marks = near_keys, near_queries, near_marks
+            if index > 0:
+                keys = pick(swaps[index], near_keys, far_keys)
+                queries = pick(swaps[index], near_queries, far_queries)
+                marks = pick(swaps[index], near_marks, far_marks)
+            first = (others[index] * n * rows + at).astype(jnp.float32)
+            twice = jnp.tanh(dot_rows(scaled_a[part], keys) + 0.5 * logit_bias)
+            twice += jnp.where(offsets[part] == first, -1.0, 1.0)
             total_a[part] += jnp.dot(
-                jnp.concatenate(key_weights, 1), all_keys, preferred_element_type=jnp.float32
+                twice.astype(jnp.bfloat16), keys, preferred_element_type=jnp.float32
             )
+            twice = jnp.tanh(dot_rows(scaled_b[part], queries) + 0.5 * logit_bias)
+            twice += jnp.where(marks - own_firsts[index] == row, -1.0, 1.0)
             total_b[part] += jnp.dot(
-                jnp.concatenate(query_weights, 1), all_queries, preferred_element_type=jnp.float32
+                twice.astype(jnp.bfloat16), queries, preferred_element_type=jnp.float32
             )
 
     def step_body(step, carry):
@@ -268,11 +281,15 @@
     lax.fori_loop(1, half + 2, step_body, 0)
 
     shares = (
-        to_mate(total_a.at[rows : 2 * rows], share_a, 2),
-        to_mate(total_b.at[rows : 2 * rows], share_b, 3),
-    )
-    for each in shares:
+        to_mate(total_a.at[2 * rows : 3 * rows], share_a, 2),
+        to_mate(total_b.at[2 * rows : 3 * rows], share_b, 3),
+    )
+    for total, each in zip((total_a, total_b), shares):
+        middle = total[part_of(1)]
+        nothing = jnp.zeros_like(middle)
+        total[part_of(2)] += pick(swap_1, middle, nothing)
         each.start()
+        total[part_of(0)] += pick(swap_1, nothing, middle)
 
     send_own(sent)
     send_crossed(sent)
@@ -314,13 +331,13 @@
             pltpu.VMEM((slots, rows, width), jnp.bfloat16),
             pltpu.VMEM((rows + EXTRA, width), jnp.bfloat16),
             pltpu.VMEM((rows, width), jnp.bfloat16),
-            pltpu.VMEM((2 * rows, width), jnp.float32),
-            pltpu.VMEM((2 * rows, width), jnp.float32),
+            pltpu.VMEM((3 * rows, width), jnp.float32),
+            pltpu.VMEM((3 * rows, width), jnp.float32),
             pltpu.VMEM((rows, width), jnp.float32),
             pltpu.VMEM((rows, width), jnp.float32),
-            pltpu.VMEM((2 * rows, width), jnp.bfloat16),
-            pltpu.VMEM((2 * rows, width), jnp.bfloat16),
-            pltpu.VMEM((2 * rows, rows), jnp.float32),
+            pltpu.VMEM((3 * rows, width), jnp.bfloat16),
+            pltpu.VMEM((3 * rows, width), jnp.bfloat16),
+            pltpu.VMEM((3 * rows, rows), jnp.float32),
             pltpu.VMEM((1, rows), jnp.int32),
             pltpu.SMEM(plan.shape, jnp.int32),
             pltpu.SemaphoreType.DMA((4,)),
@@ -335,9 +352,9 @@
             collective_id=0, has_side_effects=True, vmem_limit_bytes=60 << 20
         ),
         cost_estimate=pl.CostEstimate(
-            flops=16 * slots * rows * rows * width,
+            flops=12 * slots * rows * rows * width,
             bytes_accessed=4 * rows * width * 4,
-            transcendentals=4 * slots * rows * rows,
+            transcendentals=3 * slots * rows * rows,
         ),
     )(views_a, views_b, positives.reshape(1, rows), plan)
 

time: 47.3 us -> 47.5 us (level)
  no operation moved by 1% of the time
where the time goes in v6:
time: 47.5 us; the launch traced here: 47.3 us
  Pallas kernels  44.3 us (93%)
  local copies, waits for them, and re-layouts  2.42 us (5%)
  between operations  0.65 us (1%)
    pallas_call x1, Pallas kernels, shards(): pl.pallas_call(functools.partial(kernel, n, factor), out_shape=(out, out)...  44.3 us
    unnamed x4, local copies, waits for them, and re-layouts  2.42 us

profile of v6, /device:TPU:0, one launch (start us, length us, event | category | flops | bytes accessed | tf_op | source)
XLA Modules:
  0.0 47.3 jit_solution(4516202855435000071)
XLA Ops:
  0.6 44.3 %shard_map.59 = (f32[256,256]{1,0:T(8,128)}, f32[256,256]{1,0:T(8,128)}) custom-call(bf16[256,256]{1,0:T(8,128)(2,1)} %a_in.1, bf16[256,256]{1,0:T(8,128)(2,1)} %b_in.1, s32[1,256]{1,0:T(1,128)} %bitcast.1, s32[2,4]{1,0:T(2,128)} %plan_in.1), custom_call_target="tpu_custom_call" | custom-call | flops 3221225472 | bytes 1048576 | tf_op jit(solution)/shard_map/pallas_call | solution.py:324
  44.9 0.0 copy-start
  44.9 1.7 %copy.8 = f32[256,256]{1,0:T(8,128)} copy(f32[256,256]{1,0:T(8,128)} %get-tuple-element.4) | data formatting | bytes 524288
  46.6 0.0 copy-done
  46.6 0.7 %copy.9 = f32[256,256]{1,0:T(8,128)} copy(f32[256,256]{1,0:T(8,128)S(1)} %copy-done) | data formatting | bytes 524288
Async XLA Ops:
  44.9 1.7 %copy-start = (f32[256,256]{1,0:T(8,128)S(1)}, f32[256,256]{1,0:T(8,128)}, u32[]{:S(2)}) copy-start(f32[256,256]{1,0:T(8,128)} %get-tuple-element.5) | copy-start | bytes 786436

commit v7 on v6

--- a/solution.py
+++ b/solution.py
@@ -21,8 +21,8 @@
 
 
 def kernel(
-    n, factor, a_in, b_in, labels_in, plan_in, out_a, out_b,
-    held_a, held_b, mate_a, mate_b, total_a, total_b, share_a, share_b,
+    n, factor, a_in, b_in, labels_in, plan_in, own_a, own_b, share_a, share_b,
+    held_a, held_b, mate_a, mate_b, total_a, total_b,
     scaled_a, scaled_b, offsets, labels_held, plan,
     own_sems, recv_a, recv_b, send_a, send_b, mate_send, mate_recv,
 ):
@@ -112,6 +112,9 @@
             def _():
                 act(0, q, spot, RIGHT)
 
+            if q == 0 and half == 1:
+                act(0, q, spot, CROSS)
+
     def send_a_ahead(q, step, act, first=None):
         farthest = half - 1 + q
 
@@ -124,6 +127,12 @@
             @pl.when(step < farthest)
             def _():
                 act(0, q, spot, LEFT)
+
+            if q == 0:
+
+                @pl.when(step == 1)
+                def _():
+                    act(0, q, spot, CROSS)
 
     def send_own(act):
         act(1, 0, place, LEFT)
@@ -136,7 +145,6 @@
         act(1, 0, place, CROSS)
 
     def send_crossed(act):
-        act(0, 1, place, LEFT)
         if half > 1:
             act(0, 1, place, RIGHT)
 
@@ -284,12 +292,17 @@
         to_mate(total_a.at[2 * rows : 3 * rows], share_a, 2),
         to_mate(total_b.at[2 * rows : 3 * rows], share_b, 3),
     )
-    for total, each in zip((total_a, total_b), shares):
+    stores = (
+        pltpu.make_async_copy(total_a.at[0:rows], own_a, own_sems.at[0]),
+        pltpu.make_async_copy(total_b.at[0:rows], own_b, own_sems.at[1]),
+    )
+    for total, share, store in zip((total_a, total_b), shares, stores):
         middle = total[part_of(1)]
         nothing = jnp.zeros_like(middle)
         total[part_of(2)] += pick(swap_1, middle, nothing)
-        each.start()
+        share.start()
         total[part_of(0)] += pick(swap_1, nothing, middle)
+        store.start()
 
     send_own(sent)
     send_crossed(sent)
@@ -306,12 +319,16 @@
 
     lax.fori_loop(1, half + 1, drain_body, 0)
 
-    shares[0].wait_recv()
-    out_a[...] = (total_a[0:rows] + share_a[...]) * (0.5 * factor)
-    shares[1].wait_recv()
-    out_b[...] = (total_b[0:rows] + share_b[...]) * (0.5 * factor)
-    for each in shares:
-        each.wait_send()
+    for store in stores:
+        store.wait()
+    for share in shares:
+        share.wait_recv()
+        share.wait_send()
+
+
+def finish(factor, own_a, own_b, share_a, share_b, out_a, out_b):
+    out_a[...] = (own_a[...] + share_a[...]) * (0.5 * factor)
+    out_b[...] = (own_b[...] + share_b[...]) * (0.5 * factor)
 
 
 def shards(views_a, views_b, positives, plan):
@@ -319,13 +336,13 @@
     n = lax.axis_size("dev")
     slots = 2 * n
     factor = logit_scale / math.sqrt(width)
-    vmem = pl.BlockSpec(memory_space=pltpu.VMEM)
+    vmem, hbm = (pl.BlockSpec(memory_space=space) for space in (pltpu.VMEM, pl.ANY))
     out = jax.ShapeDtypeStruct((rows, width), jnp.float32)
-    return pl.pallas_call(
+    sums = pl.pallas_call(
         functools.partial(kernel, n, factor),
-        out_shape=(out, out),
-        in_specs=[pl.BlockSpec(memory_space=pltpu.HBM)] * 4,
-        out_specs=(vmem, vmem),
+        out_shape=(out,) * 4,
+        in_specs=[hbm] * 4,
+        out_specs=(hbm,) * 4,
         scratch_shapes=[
             pltpu.VMEM((slots, rows + EXTRA, width), jnp.bfloat16),
             pltpu.VMEM((slots, rows, width), jnp.bfloat16),
@@ -333,8 +350,6 @@
             pltpu.VMEM((rows, width), jnp.bfloat16),
             pltpu.VMEM((3 * rows, width), jnp.float32),
             pltpu.VMEM((3 * rows, width), jnp.float32),
-            pltpu.VMEM((rows, width), jnp.float32),
-            pltpu.VMEM((rows, width), jnp.float32),
             pltpu.VMEM((3 * rows, width), jnp.bfloat16),
             pltpu.VMEM((3 * rows, width), jnp.bfloat16),
             pltpu.VMEM((3 * rows, rows), jnp.float32),
@@ -357,6 +372,13 @@
             transcendentals=3 * slots * rows * rows,
         ),
     )(views_a, views_b, positives.reshape(1, rows), plan)
+    return pl.pallas_call(
+        functools.partial(finish, factor),
+        out_shape=(out, out),
+        in_specs=[vmem] * 4,
+        out_specs=(vmem, vmem),
+        compiler_params=pltpu.CompilerParams(vmem_limit_bytes=60 << 20),
+    )(*sums)
 
 
 def solution(mesh):

time: 47.5 us -> 45.6 us (0.960)
  local copies, waits for them, and re-layouts: 2.42 us -> 0 us
  Pallas kernels: 44.3 us -> 44.8 us
    unnamed x4 -> x0, local copies, waits for them, and re-layouts: 2.42 us -> none
    pallas_call x1 -> x2, Pallas kernels: 44.3 us -> 44.8 us  [the longest x1 42.8 us: shards(): pl.pallas_call(functools.partial(kernel, n, factor), out_shape=(out,) * 4...]
where the time goes in v7:
time: 45.6 us; the launch traced here: 45.4 us
  Pallas kernels  44.8 us (98%)
  between operations  0.64 us (1%)
    pallas_call x1, Pallas kernels, shards(): pl.pallas_call(functools.partial(kernel, n, factor), out_shape=(out,) * 4...  42.8 us
    pallas_call x1, Pallas kernels, shards(): pl.pallas_call(functools.partial(finish, factor), out_shape=(out, out), i...  2.01 us

profile of v7, /device:TPU:0, one launch (start us, length us, event | category | flops | bytes accessed | tf_op | source)
XLA Modules:
  0.0 45.4 jit_solution(11464505232160778934)
XLA Ops:
  0.6 42.8 %shard_map.59 = (f32[256,256]{1,0:T(8,128)}, f32[256,256]{1,0:T(8,128)}, f32[256,256]{1,0:T(8,128)}, f32[256,256]{1,0:T(8,128)}) custom-call(bf16[256,256]{1,0:T(8,128)(2,1)} %a_in.1, bf16[256,256]{1,0:T(8,128)(2,1)} %b_in.1, s32[1,256]{1,0:T(1,128)} %bitcast.1, s32[2,4]{1,0:T(2,128)} %plan_in.1), custom_call_target="tpu_custom_call" | custom-call | flops 3221225472 | bytes 1048576 | tf_op jit(solution)/shard_map/pallas_call | solution.py:341
  43.4 2.0 %shard_map.60 = (f32[256,256]{1,0:T(8,128)}, f32[256,256]{1,0:T(8,128)}) custom-call(f32[256,256]{1,0:T(8,128)} %get-tuple-element.6.own_a, f32[256,256]{1,0:T(8,128)} %get-tuple-element.7.own_b, f32[256,256]{1,0:T(8,128)} %get-tuple-element.8.share_a, f32[256,256]{1,0:T(8,128)} %get-tuple-element.9.share_b), custom_call_target="tpu_custom_call" | custom-call | tf_op jit(solution)/shard_map/pallas_call | solution.py:375

commit v8 on v7

--- a/solution.py
+++ b/solution.py
@@ -134,11 +134,12 @@
                 def _():
                     act(0, q, spot, CROSS)
 
-    def send_own(act):
+    def send_own_first(act):
         act(1, 0, place, LEFT)
         if half > 1:
             act(1, 0, place, RIGHT)
-        act(0, 0, place, CROSS)
+
+    def send_own_then(act):
         act(0, 0, place, RIGHT)
         if half > 1:
             act(0, 0, place, LEFT)
@@ -180,7 +181,8 @@
     coded = jnp.where(line == 0, high, jnp.where(line == 1, low, 0.0))
     held_a[mine, rows : rows + EXTRA, :] = coded.astype(jnp.bfloat16)
     pl.semaphore_wait(barrier, 4)
-    send_own(start)
+    send_own_first(start)
+    start(0, 0, place, CROSS)
     own_to_mate = (
         to_mate(held_a.at[mine], mate_a, 0),
         to_mate(held_b.at[mine], mate_b, 1),
@@ -219,6 +221,8 @@
     total_a[...] = jnp.zeros_like(total_a)
     total_b[...] = jnp.zeros_like(total_b)
 
+    send_own_first(sent)
+    send_own_then(start)
     arrived(0, 1, place)
     send_crossed(start)
     for each in own_to_mate:
@@ -304,7 +308,8 @@
         total[part_of(0)] += pick(swap_1, nothing, middle)
         store.start()
 
-    send_own(sent)
+    sent(0, 0, place, CROSS)
+    send_own_then(sent)
     send_crossed(sent)
     for each in own_to_mate:
         each.wait_send()

time: 45.6 us -> 46 us (level)
  no operation moved by 1% of the time
where the time goes in v8:
time: 46 us; the launch traced here: 45.6 us
  Pallas kernels  45 us (98%)
  between operations  0.64 us (1%)
    pallas_call x1, Pallas kernels, shards(): pl.pallas_call(functools.partial(kernel, n, factor), out_shape=(out,) * 4...  43 us
    pallas_call x1, Pallas kernels, shards(): pl.pallas_call(functools.partial(finish, factor), out_shape=(out, out), i...  2.01 us

profile of v8, /device:TPU:0, one launch (start us, length us, event | category | flops | bytes accessed | tf_op | source)
XLA Modules:
  0.0 45.6 jit_solution(13138214347244842369)
XLA Ops:
  0.6 43.0 %shard_map.59 = (f32[256,256]{1,0:T(8,128)}, f32[256,256]{1,0:T(8,128)}, f32[256,256]{1,0:T(8,128)}, f32[256,256]{1,0:T(8,128)}) custom-call(bf16[256,256]{1,0:T(8,128)(2,1)} %a_in.1, bf16[256,256]{1,0:T(8,128)(2,1)} %b_in.1, s32[1,256]{1,0:T(1,128)} %bitcast.1, s32[2,4]{1,0:T(2,128)} %plan_in.1), custom_call_target="tpu_custom_call" | custom-call | flops 3221225472 | bytes 1048576 | tf_op jit(solution)/shard_map/pallas_call | solution.py:346
  43.6 2.0 %shard_map.60 = (f32[256,256]{1,0:T(8,128)}, f32[256,256]{1,0:T(8,128)}) custom-call(f32[256,256]{1,0:T(8,128)} %get-tuple-element.6.own_a, f32[256,256]{1,0:T(8,128)} %get-tuple-element.7.own_b, f32[256,256]{1,0:T(8,128)} %get-tuple-element.8.share_a, f32[256,256]{1,0:T(8,128)} %get-tuple-element.9.share_b), custom_call_target="tpu_custom_call" | custom-call | tf_op jit(solution)/shard_map/pallas_call | solution.py:380

commit v9 on v7

--- a/solution.py
+++ b/solution.py
@@ -277,13 +277,22 @@
                 send_b_behind(2 * step, start, arrived)
                 send_b_ahead(2 * step, start, arrived)
 
+                @pl.when(step < half)
+                def _():
+                    send_a_behind(1, step, start, arrived)
+                    send_a_ahead(1, step, start, arrived)
+
             return carry
 
         send_b_behind(2 * step - 1, start, arrived)
         send_b_ahead(2 * step - 1, start, arrived)
         lax.fori_loop(0, count, turn, 0)
-        send_a_behind(1, step, start, arrived)
-        send_a_ahead(1, step, start, arrived)
+
+        @pl.when(step == half)
+        def _():
+            send_a_behind(1, step, start, arrived)
+            send_a_ahead(1, step, start, arrived)
+
         return carry
 
     lax.fori_loop(1, half + 2, step_body, 0)

time: 45.6 us -> 45.8 us (level)
  no operation moved by 1% of the time
where the time goes in v9:
time: 45.8 us; the launch traced here: 45.7 us
  Pallas kernels  45 us (98%)
  between operations  0.64 us (1%)
    pallas_call x1, Pallas kernels, shards(): pl.pallas_call(functools.partial(kernel, n, factor), out_shape=(out,) * 4...  43 us
    pallas_call x1, Pallas kernels, shards(): pl.pallas_call(functools.partial(finish, factor), out_shape=(out, out), i...  2.01 us

profile of v9, /device:TPU:0, one launch (start us, length us, event | category | flops | bytes accessed | tf_op | source)
XLA Modules:
  0.0 45.7 jit_solution(1567288293810299229)
XLA Ops:
  0.6 43.0 %shard_map.59 = (f32[256,256]{1,0:T(8,128)}, f32[256,256]{1,0:T(8,128)}, f32[256,256]{1,0:T(8,128)}, f32[256,256]{1,0:T(8,128)}) custom-call(bf16[256,256]{1,0:T(8,128)(2,1)} %a_in.1, bf16[256,256]{1,0:T(8,128)(2,1)} %b_in.1, s32[1,256]{1,0:T(1,128)} %bitcast.1, s32[2,4]{1,0:T(2,128)} %plan_in.1), custom_call_target="tpu_custom_call" | custom-call | flops 3221225472 | bytes 1048576 | tf_op jit(solution)/shard_map/pallas_call | solution.py:350
  43.7 2.0 %shard_map.60 = (f32[256,256]{1,0:T(8,128)}, f32[256,256]{1,0:T(8,128)}) custom-call(f32[256,256]{1,0:T(8,128)} %get-tuple-element.6.own_a, f32[256,256]{1,0:T(8,128)} %get-tuple-element.7.own_b, f32[256,256]{1,0:T(8,128)} %get-tuple-element.8.share_a, f32[256,256]{1,0:T(8,128)} %get-tuple-element.9.share_b), custom_call_target="tpu_custom_call" | custom-call | tf_op jit(solution)/shard_map/pallas_call | solution.py:384
